TPU v7x, 32 devices: a whole 2x2x4 slice. The times are simulated.
32 devices in a mesh: tm: 4 (over x, core), tmpl: 8 (over z, y).
Axes of the slice: x: 2, y: 2, z: 4, core: 2. Of those that a mesh axis runs over, the one named last changes fastest.
Arguments:
- strain: float32 [2, 786432], P(None, 'tm'), may hold values from -24 to 24
- segment_valid: int32 [2, 3072], P(None, 'tm'), may hold values 0 or 1
- templates: float32 [16, 512], P('tmpl'), may hold values from -6 to 6
- durations: int32 [16], P('tmpl'), may hold values from 128 to 512
- bin_edges: int32 [16, 15], P('tmpl'), may hold values from 1 to 255, as said below
Outputs:
- peaks: float32 [5, 786432], P(None, ('tm', 'tmpl'))
Inputs may be any that keep to these rules, and one draw needn't show every extreme that they name: `bin_edges`: each row holds 15 bin edges in strictly increasing order.
All inputs are finite; a program needn't handle non-finite values. No bound on the sum of `segment_valid` on one device may be relied on, other than what follows from the above.
Results may differ from a plain program's by a relative error of at most 0.0014.
Values sent between devices are 32-bit elements; how exact they have to be, the bound alone decides.
A program may use at most 64 MiB of HBM per device.

v0:
```python
import math

import jax
import jax.numpy as jnp
import numpy as np
from jax import lax
from jax.experimental import pallas as pl
from jax.experimental.pallas import tpu as pltpu
from jax.sharding import PartitionSpec as P

DET = 2
BLOCK = 1024
TLEN = 512
STRIDE = 512
FBAND = 256
FLOW = 4
BINS = 16
SEG = 256
POINTS = 128
NARROW = POINTS // 2
EXTRA = 8
GROUP = 4
MESH = pl.DeviceIdType.MESH

epsilon = 1e-06


def forward_table():
    frequency = FLOW + np.arange(FBAND)
    phase = np.arange(STRIDE)[:, None] * frequency[None, :] % BLOCK
    angles = np.float32(2.0 * math.pi / BLOCK) * phase.astype(np.float32)
    factor = np.float32(1.0 / math.sqrt(BLOCK))
    return np.concatenate([np.cos(angles), -np.sin(angles)], axis=1) * factor


def rotation_table(frequency, offset, period):
    phase = frequency[:, None] * offset[None, :] % period
    angles = np.float32(2.0 * math.pi / period) * phase.astype(np.float32)
    cosine, sine = np.cos(angles), np.sin(angles)
    upper = np.concatenate([cosine, sine], axis=1)
    lower = np.concatenate([-sine, cosine], axis=1)
    return np.concatenate([upper, lower], axis=0)


def spread_table():
    step = BLOCK // POINTS
    delta = np.arange(STRIDE)[None, :] - step * np.arange(POINTS)[:, None]
    lags = np.arange(1, NARROW)
    waves = np.cos(2.0 * math.pi / BLOCK * (delta[:, :, None] * lags % BLOCK))
    table = (1.0 + 2.0 * waves.sum(axis=2)) / POINTS
    return np.concatenate([table, table], axis=0)


def prepare(n_tm, n_tp, blocks, x_ref, valid_ref, edge_ref, table_ref, spec_ref, filt_ref,
            sig_ref, cut_ref, g_ref, head, halo, pack, part, whole, halo_sem, pack_send,
            pack_recv, part_send, part_recv, whole_send, whole_recv):
    me_tm, me_tp = lax.axis_index("tm"), lax.axis_index("tmpl")
    rows = DET * blocks
    halo[...] = jnp.zeros_like(halo)
    barrier = pltpu.get_barrier_semaphore()
    for r in range(1, n_tp):
        pl.semaphore_signal(barrier, inc=1, device_id=(me_tm, lax.rem(me_tp + r, n_tp)),
                            device_id_type=MESH)
    for r in range(1, n_tm):
        pl.semaphore_signal(barrier, inc=1, device_id=(lax.rem(me_tm + r, n_tm), me_tp),
                            device_id_type=MESH)
    valid = valid_ref[...]
    lane = lax.broadcasted_iota(jnp.int32, x_ref.shape, 1)
    gate = jnp.where(lane < SEG, valid[:, :1], valid[:, 1:2])
    g = jnp.dot(x_ref[...] * gate, table_ref[...], precision=lax.Precision.HIGHEST,
                preferred_element_type=jnp.float32)
    for d in range(DET):
        g_ref[d, :blocks, :] = g[d * blocks:(d + 1) * blocks]
        g_ref[d, blocks:blocks + 1, :] = g[rows + d:rows + d + 1]
    head[...] = g[rows + DET:rows + 2 * DET]
    pack[0, :, :2 * FBAND] = g[rows + 2 * DET:rows + 2 * DET + 2]
    pack[0, :, 2 * FBAND:] = edge_ref[...]
    pl.semaphore_wait(barrier, n_tp + n_tm - 2)

    last = me_tp == n_tp - 1

    def halo_copy():
        return pltpu.make_async_remote_copy(
            src_ref=head, dst_ref=halo, send_sem=halo_sem.at[0], recv_sem=halo_sem.at[1],
            device_id=(lax.rem(me_tm + n_tm - 1, n_tm), me_tp), device_id_type=MESH)

    @pl.when(jnp.logical_and(last, me_tm > 0))
    def _():
        halo_copy().start()

    packs = []
    for r in range(1, n_tp):
        packs.append(pltpu.make_async_remote_copy(
            src_ref=pack.at[0], dst_ref=pack.at[r], send_sem=pack_send.at[r],
            recv_sem=pack_recv.at[r], device_id=(me_tm, lax.rem(me_tp + r, n_tp)),
            device_id_type=MESH))
        packs[-1].start()

    @pl.when(jnp.logical_and(last, me_tm < n_tm - 1))
    def _():
        halo_copy().wait_recv()

    @pl.when(last)
    def _():
        for d in range(DET):
            g_ref[d, blocks:blocks + 1, :] = halo[d:d + 1, :]

    column = lax.broadcasted_iota(jnp.int32, (1, 2 * FBAND), 1)
    sign = jnp.where(column % 2 == 0, 1.0, -1.0)
    for d in range(DET):
        s = g_ref[d, :blocks, :] + sign * g_ref[d, 1:blocks + 1, :]
        spec_ref[d * blocks:(d + 1) * blocks, :] = s
        power = jnp.sum(s * s, axis=0, keepdims=True)
        part[0, d:d + 1, :] = power[:, :FBAND] + power[:, FBAND:]

    parts = []
    for r in range(1, n_tp):
        parts.append(pltpu.make_async_remote_copy(
            src_ref=part.at[0], dst_ref=part.at[r], send_sem=part_send.at[r],
            recv_sem=part_recv.at[r], device_id=(me_tm, lax.rem(me_tp + r, n_tp)),
            device_id_type=MESH))
        parts[-1].start()
    for copy in parts:
        copy.wait_recv()
    total = part[0]
    for r in range(1, n_tp):
        total = total + part[r]
    whole[0] = total
    wholes = []
    for r in range(1, n_tm):
        wholes.append(pltpu.make_async_remote_copy(
            src_ref=whole.at[0], dst_ref=whole.at[r], send_sem=whole_send.at[r],
            recv_sem=whole_recv.at[r], device_id=(lax.rem(me_tm + r, n_tm), me_tp),
            device_id_type=MESH))
        wholes[-1].start()
    for copy in packs:
        copy.wait_recv()
    for copy in wholes:
        copy.wait_recv()
    total = whole[0]
    for r in range(1, n_tm):
        total = total + whole[r]
    weight = 1.0 / (total / (blocks * n_tp * n_tm) + epsilon)
    for r in range(n_tp):
        for i in range(2):
            re, im = pack[r, i:i + 1, :FBAND], pack[r, i:i + 1, FBAND:2 * FBAND]
            filt_ref[2 * r + i, :, :FBAND] = re * weight
            filt_ref[2 * r + i, :, FBAND:] = -im * weight
            sigma = jnp.sum((re * re + im * im) * weight, axis=1, keepdims=True)
            sig_ref[2 * r + i] = jnp.broadcast_to(1.0 / sigma, (DET, 128))
        cut_ref[r] = pack[r, :, 2 * FBAND:].astype(jnp.int32)
    for copy in packs + parts + wholes:
        copy.wait_send()

    @pl.when(jnp.logical_and(last, me_tm > 0))
    def _():
        halo_copy().wait_send()


def score(count, blocks, cut_ref, spec_ref, filt_ref, sig_ref, inverse_ref, sample_ref,
          spread_ref, out_ref, prod, lhs, best, squares_a, squares_b, mag_a, mag_b, turned):
    rows = DET * blocks
    best[...] = jnp.zeros_like(best)

    def fill(j, g):
        filt = filt_ref[j]
        for d in range(DET):
            own = slice(d * blocks, (d + 1) * blocks)
            to = slice(g * rows + d * blocks, g * rows + (d + 1) * blocks)
            sr, si = spec_ref[own, :FBAND], spec_ref[own, FBAND:]
            fr, fi = filt[d:d + 1, :FBAND], filt[d:d + 1, FBAND:]
            prod[to, :FBAND] = (sr * fr - si * fi).astype(jnp.bfloat16)
            prod[to, FBAND:] = (sr * fi + si * fr).astype(jnp.bfloat16)
        product = prod[g * rows:(g + 1) * rows, :]
        edges = [0] + [cut_ref[j, p] for p in range(BINS - 1)] + [FBAND]
        lane = lax.broadcasted_iota(jnp.int32, (16, 128), 1)
        copies = rows // 16
        widest = 0
        for p in range(BINS):
            low, high = edges[p], edges[p + 1]
            widest = jnp.maximum(widest, high - low)
            high = jnp.where(high - low > NARROW, low, high)
            masks = [
                jnp.where((lane + k >= low) & (lane + k < high), 1.0, 0.0).astype(jnp.bfloat16)
                for k in (0, 128)
            ]
            masks = [jnp.concatenate([mask] * copies, axis=0) for mask in masks]
            part = slice((p * GROUP + g) * rows, (p * GROUP + g + 1) * rows)
            lhs[part, :128] = product[:, :128] * masks[0] + product[:, 128:256] * masks[1]
            lhs[part, 128:] = product[:, 256:384] * masks[0] + product[:, 384:] * masks[1]
        return widest

    def produce(j, squares, mag):
        widest = []
        for g in range(GROUP):
            widest.append(fill(j + g, g))
        product = prod[...]
        corr = jnp.dot(product, inverse_ref[...], preferred_element_type=jnp.float32)
        corr = corr * corr
        mag[...] = corr[:, :STRIDE] + corr[:, STRIDE:]
        points = jnp.dot(lhs[...], sample_ref[...], preferred_element_type=jnp.float32)
        points = points * points
        points = (points[:, :POINTS] + points[:, POINTS:]).reshape(BINS, GROUP * rows, POINTS)
        total = jnp.sum(points, axis=0)
        upper = total.astype(jnp.bfloat16)
        lower = (total - upper.astype(jnp.float32)).astype(jnp.bfloat16)
        squares[...] = jnp.dot(jnp.concatenate([upper, lower], axis=1), spread_ref[...],
                               preferred_element_type=jnp.float32)
        return widest

    def add_wide(j, widest, squares):
        for g in range(GROUP):
            own = slice(g * rows, (g + 1) * rows)

            @pl.when(widest[g] > NARROW)
            def _():
                def one_bin(p, carry):
                    low = jnp.where(p == 0, 0, cut_ref[j + g, jnp.maximum(p - 1, 0)])
                    high = jnp.where(
                        p == BINS - 1, FBAND, cut_ref[j + g, jnp.minimum(p, BINS - 2)])

                    @pl.when(high - low > NARROW)
                    def _():
                        column = lax.broadcasted_iota(jnp.int32, (1, 2 * FBAND), 1) % FBAND
                        mask = jnp.where((column >= low) & (column < high), 1.0, 0.0)
                        masked = prod[own, :] * mask.astype(jnp.bfloat16)
                        z = jnp.dot(masked, inverse_ref[...], preferred_element_type=jnp.float32)
                        z = z * z
                        squares[own, :] += BINS * (z[:, :STRIDE] + z[:, STRIDE:])

                    return carry

                lax.fori_loop(0, BINS, one_bin, 0)

    def consume(j, squares, mag):
        for g in range(GROUP):
            network = None
            for d in range(DET):
                own = slice(g * rows + d * blocks, g * rows + (d + 1) * blocks)
                scale = sig_ref[j + g][d:d + 1, :1]
                strength = mag[own, :] * scale
                reduced = (squares[own, :] - mag[own, :]) * (scale * (1.0 / (2.0 * BINS - 2.0)))
                reduced = jnp.maximum(reduced, 1.0)
                cube = reduced * reduced * reduced + 1.0
                weighted = strength * jnp.exp2(jnp.log(cube) * (-1.0 / (3.0 * math.log(2.0))))
                best[d] = jnp.maximum(best[d], strength)
                best[DET + d] = jnp.maximum(best[DET + d], weighted)
                network = weighted if network is None else network + weighted
            best[2 * DET] = jnp.maximum(best[2 * DET], network)

    def step(i, now, later):
        consume(i * GROUP, *now)
        widest = produce((i + 1) * GROUP, *later)
        add_wide((i + 1) * GROUP, widest, later[0])

    slot_a, slot_b = (squares_a, mag_a), (squares_b, mag_b)
    add_wide(0, produce(0, *slot_a), squares_a)

    def pair(i, carry):
        step(2 * i, slot_a, slot_b)
        step(2 * i + 1, slot_b, slot_a)
        return carry

    groups = count // GROUP
    lax.fori_loop(0, (groups - 1) // 2, pair, 0)
    if groups % 2 == 0:
        step(groups - 2, slot_a, slot_b)
        consume(count - GROUP, *slot_b)
    else:
        consume(count - GROUP, *slot_a)
    for d in range(2 * DET + 1):
        gain = 1.0 if d < DET else 2.0 ** (1.0 / 6.0)
        root = jnp.sqrt(best[d]) * gain
        for c in range(STRIDE // 128):
            turned[c, pl.ds(d, blocks, stride=8), :] = root[:, c * 128:(c + 1) * 128]
    for b in range(blocks):
        for c in range(STRIDE // 128):
            at = b * STRIDE + c * 128
            out_ref[:, at:at + 128] = turned[c, 8 * b:8 * b + 2 * DET + 1, :]


def scoring_call(count, blocks):
    f32 = jnp.float32
    rows = DET * blocks
    vmem = pl.BlockSpec(memory_space=pltpu.VMEM)

    def scoring(*refs):
        score(count, blocks, *refs)

    return pl.pallas_call(
        scoring,
        out_shape=jax.ShapeDtypeStruct((2 * DET + 1, blocks * STRIDE), f32),
        in_specs=[pl.BlockSpec(memory_space=pltpu.SMEM)] + [vmem] * 6,
        out_specs=vmem,
        scratch_shapes=[
            pltpu.VMEM((GROUP * rows, 2 * FBAND), jnp.bfloat16),
            pltpu.VMEM((BINS * GROUP * rows, 2 * POINTS), jnp.bfloat16),
            pltpu.VMEM((2 * DET + 1, blocks, STRIDE), f32),
            pltpu.VMEM((GROUP * rows, STRIDE), f32), pltpu.VMEM((GROUP * rows, STRIDE), f32),
            pltpu.VMEM((GROUP * rows, STRIDE), f32), pltpu.VMEM((GROUP * rows, STRIDE), f32),
            pltpu.VMEM((STRIDE // 128, 8 * blocks, 128), f32),
        ],
        compiler_params=pltpu.CompilerParams(vmem_limit_bytes=40 * 2**20),
    )


def scoring_tables():
    inverse = rotation_table(FLOW + np.arange(FBAND), np.arange(STRIDE), BLOCK)
    sample = rotation_table(np.arange(POINTS), np.arange(POINTS), POINTS)
    spread = BINS * spread_table()
    return [jnp.asarray(table.astype(jnp.bfloat16)) for table in (inverse, sample, spread)]


def shards(strain, segment_valid, templates, durations, bin_edges):
    n_tm, n_tp = lax.axis_size("tm"), lax.axis_size("tmpl")
    me_tp = lax.axis_index("tmpl")
    span_len = strain.shape[1]
    piece = span_len // n_tp
    blocks = piece // STRIDE
    rows = DET * blocks
    per = templates.shape[0]
    count = per * n_tp
    pick = STRIDE // SEG

    start = me_tp * piece
    follow = lax.rem(me_tp + 1, n_tp) * piece
    own = lax.dynamic_slice_in_dim(strain, start, piece, 1).reshape(rows, STRIDE)
    next_block = lax.dynamic_slice_in_dim(strain, follow, STRIDE, 1)
    within = jnp.arange(TLEN, dtype=jnp.int32)[None, :] < durations[:, None]
    shaped = jnp.where(within, templates, 0.0)
    spare = EXTRA - 2 * DET - per
    x = jnp.concatenate(
        [own, next_block, strain[:, :STRIDE], shaped, jnp.zeros((spare, STRIDE), jnp.float32)])
    own_valid = lax.dynamic_slice_in_dim(segment_valid, start // SEG, pick * blocks, 1)
    next_valid = lax.dynamic_slice_in_dim(segment_valid, follow // SEG, pick, 1)
    valid = jnp.concatenate(
        [own_valid.reshape(rows, pick), next_valid, segment_valid[:, :pick],
         jnp.ones((per + spare, pick), jnp.int32)]).astype(jnp.float32)
    edges = jnp.pad(bin_edges.astype(jnp.float32), ((0, 0), (0, 128 - bin_edges.shape[1])))

    vmem = pl.BlockSpec(memory_space=pltpu.VMEM)
    dma = pltpu.SemaphoreType.DMA
    f32 = jnp.float32

    def body(*refs):
        prepare(n_tm, n_tp, blocks, *refs)

    spec, filt, sig, cut = pl.pallas_call(
        body,
        out_shape=(
            jax.ShapeDtypeStruct((rows, 2 * FBAND), f32),
            jax.ShapeDtypeStruct((count, DET, 2 * FBAND), f32),
            jax.ShapeDtypeStruct((count, DET, 128), f32),
            jax.ShapeDtypeStruct((n_tp, per, 128), jnp.int32),
        ),
        in_specs=[vmem] * 4,
        out_specs=(vmem,) * 4,
        scratch_shapes=[
            pltpu.VMEM((DET, blocks + 8, 2 * FBAND), f32),
            pltpu.VMEM((DET, 2 * FBAND), f32),
            pltpu.VMEM((DET, 2 * FBAND), f32),
            pltpu.VMEM((n_tp, per, 2 * FBAND + 128), f32),
            pltpu.VMEM((n_tp, DET, FBAND), f32),
            pltpu.VMEM((n_tm, DET, FBAND), f32),
            dma((2,)), dma((n_tp,)), dma((n_tp,)), dma((n_tp,)), dma((n_tp,)),
            dma((n_tm,)), dma((n_tm,)),
        ],
        compiler_params=pltpu.CompilerParams(
            collective_id=0, has_side_effects=True, vmem_limit_bytes=40 * 2**20),
    )(x, valid, edges, jnp.asarray(forward_table()))

    return scoring_call(count, blocks)(
        cut.reshape(count, 128)[:, :BINS], spec, filt, sig, *scoring_tables())


def solution(mesh):
    placed = (P(None, "tm"), P(None, "tm"), P("tmpl", None), P("tmpl"), P("tmpl", None))
    return jax.shard_map(
        shards, mesh=mesh, in_specs=placed, out_specs=P(None, ("tm", "tmpl")), check_vma=False
    )
```

profile of v0, /device:TPU:0, one launch (start us, length us, event | category | flops | bytes accessed | tf_op | source)
XLA Modules:
  0.0 32.6 jit_solution(6482832261491380955)
XLA Ops:
  0.0 0.0 copy-start.1
  0.0 0.0 copy-start.2
  0.0 0.0 copy-start.3
  0.0 0.0 copy-start
  0.0 0.9 %constant_dynamic-slice_fusion.1 = s32[2,96]{1,0:T(2,128)S(1)} fusion(s32[2,768]{1,0:T(2,128)} %param.10, s32[]{:T(128)S(6)} %select_n.28), kind=kLoop, calls=%fused_computation.3 | loop fusion | bytes 1540 | tf_op jit(solution)/shard_map/dynamic_slice | solution.py:334
  0.9 0.1 pad.8.clone
  1.0 0.7 %convert_element_type.9 = f32[2,15]{1,0:T(2,128)S(1)} convert(s32[2,15]{1,0:T(2,128)} %param.13) | non-fusion elementwise | flops 30 | bytes 240 | tf_op jit(solution)/shard_map/convert_element_type | solution.py:339
  1.7 0.8 %constant_dynamic-slice_fusion = (s32[2,2]{1,0:T(2,128)S(1)}, s32[2,2]{1,0:T(2,128)S(1)}) fusion(s32[2,768]{1,0:T(2,128)} %param.10, s32[]{:T(128)S(6)} %select_n.30), kind=kLoop, calls=%fused_computation.2 | loop fusion | bytes 68 | tf_op jit(solution)/shard_map/dynamic_slice | solution.py:335
  2.5 0.8 %fusion = (f32[2,512]{1,0:T(2,128)S(1)}, f32[2,512]{1,0:T(2,128)S(1)}, f32[2,512]{1,0:T(2,128)S(1)}) fusion(f32[2,196608]{1,0:T(2,128)} %param.9, s32[]{:T(128)S(6)} %select_n.25, f32[2,512]{1,0:T(2,128)} %param.11, s32[2]{0:T(128)} %param.12), kind=kLoop, calls=%fused_computation.6 | loop fusion | flops 2048 | bytes 24588 | tf_op jit(solution)/shard_map/slice | solution.py:333
  3.3 0.1 reshape.11
  3.4 0.1 add_convert_fusion.refs_1_
  3.5 0.9 %constant_dynamic-slice_fusion.3 = f32[2,24576]{1,0:T(2,128)S(1)} fusion(f32[2,196608]{1,0:T(2,128)} %param.9, s32[]{:T(128)S(6)} %select_n.24), kind=kLoop, calls=%fused_computation.5 | loop fusion | bytes 393220 | tf_op jit(solution)/shard_map/dynamic_slice | solution.py:327
  4.5 0.2 reshape.10
  4.7 0.0 copy-done.1
  4.7 12.8 %shard_map.91 = (f32[96,512]{1,0:T(8,128)S(1)}, f32[16,2,512]{2,1,0:T(2,128)S(1)}, f32[16,2,128]{2,1,0:T(2,128)S(1)}, s32[8,2,128]{2,1,0:T(2,128)S(1)}) custom-call(f32[104,512]{1,0:T(8,128)S(1)} %concatenate.6.refs_0_, f32[104,2]{1,0:T(8,128)S(1)} %add_convert_fusion.refs_1_, f32[2,128]{1,0:T(2,128)S(1)} %pad.4.refs_2_, f32[512,512]{1,0:T(8,128)S(1)} %copy-done.1), custom_call_target="tpu_custom_call" | custom-call | tf_op jit(solution)/shard_map/pallas_call | solution.py:348
  17.5 0.0 copy-done.2
  17.5 0.0 copy-done.3
  17.5 0.0 copy-done
  17.5 15.0 %shard_map.92 = f32[5,24576]{1,0:T(8,128)} custom-call(s32[16,16]{1,0:T(8,128)S(1)} %bitcast.2, f32[96,512]{1,0:T(8,128)S(1)} %get-tuple-element.10.refs_1_, f32[16,2,512]{2,1,0:T(2,128)S(1)} %get-tuple-element.11.refs_2_, f32[16,2,128]{2,1,0:T(2,128)S(1)} %get-tuple-element.12.refs_3_, bf16[512,1024]{1,0:T(8,128)(2,1)S(1)} %copy-done, ...), custom_call_target="tpu_custom_call" | custom-call | tf_op jit(solution)/shard_map/pallas_call | solution.py:372
  (4 shorter events, 0.1 us)
Async XLA Ops:
  0.0 4.7 %copy-start.1 = (f32[512,512]{1,0:T(8,128)S(1)}, f32[512,512]{1,0:T(8,128)}, u32[]{:S(2)}) copy-start(f32[512,512]{1,0:T(8,128)} %constant.52.clone.refs_3_) | copy-start | bytes 3145732
  0.0 17.5 %copy-start.2 = (bf16[256,512]{1,0:T(8,128)(2,1)S(1)}, bf16[256,512]{1,0:T(8,128)(2,1)}, u32[]{:S(2)}) copy-start(bf16[256,512]{1,0:T(8,128)(2,1)} %constant.55.clone.refs_6_) | copy-start | bytes 786436
  0.0 17.5 %copy-start.3 = (bf16[256,256]{1,0:T(8,128)(2,1)S(1)}, bf16[256,256]{1,0:T(8,128)(2,1)}, u32[]{:S(2)}) copy-start(bf16[256,256]{1,0:T(8,128)(2,1)} %constant.54.clone.refs_5_) | copy-start | bytes 393220
  0.0 17.5 %copy-start = (bf16[512,1024]{1,0:T(8,128)(2,1)S(1)}, bf16[512,1024]{1,0:T(8,128)(2,1)}, u32[]{:S(2)}) copy-start(bf16[512,1024]{1,0:T(8,128)(2,1)} %constant.53.clone.refs_4_) | copy-start | bytes 3145732
where the time goes:
time: 32.7 us; the launch traced here: 32.6 us
  Pallas kernels  27.8 us (85%)
  local copies, waits for them, and re-layouts  3.11 us (10%)
  other arithmetic  1.56 us (5%)
    pallas_call x1, Pallas kernels, shards(): scoring_call(count, blocks)  15 us
    pallas_call x1, Pallas kernels, shards(): pl.pallas_call(body, out_shape=(jax.ShapeDtypeStruct((rows, 2 * FBAND), f...  12.8 us
    dynamic_slice x1, local copies, waits for them, and re-layouts, shards(): lax.dynamic_slice_in_dim(strain, start, piece, 1).reshape(rows, STRIDE)  0.95 us
    dynamic_slice x1, local copies, waits for them, and re-layouts, shards(): lax.dynamic_slice_in_dim(segment_valid, start // SEG, pick * blocks, 1)  0.91 us
    dynamic_slice x1, local copies, waits for them, and re-layouts, shards(): next_valid = lax.dynamic_slice_in_dim(segment_valid, follow // SEG, pick, 1)  0.83 us
    slice x1, other arithmetic, shards(): strain[:, :STRIDE]  0.79 us
    convert_element_type x1, other arithmetic, shards(): bin_edges.astype(jnp.float32)  0.68 us

commit v1 on v0

--- a/solution.py
+++ b/solution.py
@@ -18,7 +18,7 @@
 SEG = 256
 POINTS = 128
 NARROW = POINTS // 2
-EXTRA = 8
+EXTRA = 16
 GROUP = 4
 MESH = pl.DeviceIdType.MESH
 
@@ -31,6 +31,12 @@
     angles = np.float32(2.0 * math.pi / BLOCK) * phase.astype(np.float32)
     factor = np.float32(1.0 / math.sqrt(BLOCK))
     return np.concatenate([np.cos(angles), -np.sin(angles)], axis=1) * factor
+
+
+def split_table(table):
+    upper = table.astype(jnp.bfloat16)
+    lower = (table - upper.astype(np.float32)).astype(jnp.bfloat16)
+    return np.stack([upper, lower])
 
 
 def rotation_table(frequency, offset, period):
@@ -67,8 +73,12 @@
     valid = valid_ref[...]
     lane = lax.broadcasted_iota(jnp.int32, x_ref.shape, 1)
     gate = jnp.where(lane < SEG, valid[:, :1], valid[:, 1:2])
-    g = jnp.dot(x_ref[...] * gate, table_ref[...], precision=lax.Precision.HIGHEST,
-                preferred_element_type=jnp.float32)
+    gated = x_ref[...] * gate
+    upper = gated.astype(jnp.bfloat16)
+    lower = (gated - upper.astype(jnp.float32)).astype(jnp.bfloat16)
+    g = jnp.dot(upper, table_ref[0], preferred_element_type=jnp.float32)
+    g += jnp.dot(upper, table_ref[1], preferred_element_type=jnp.float32)
+    g += jnp.dot(lower, table_ref[0], preferred_element_type=jnp.float32)
     for d in range(DET):
         g_ref[d, :blocks, :] = g[d * blocks:(d + 1) * blocks]
         g_ref[d, blocks:blocks + 1, :] = g[rows + d:rows + d + 1]
@@ -367,7 +377,7 @@
         ],
         compiler_params=pltpu.CompilerParams(
             collective_id=0, has_side_effects=True, vmem_limit_bytes=40 * 2**20),
-    )(x, valid, edges, jnp.asarray(forward_table()))
+    )(x, valid, edges, jnp.asarray(split_table(forward_table())))
 
     return scoring_call(count, blocks)(
         cut.reshape(count, 128)[:, :BINS], spec, filt, sig, *scoring_tables())

time: 32.7 us -> 31.8 us (0.972); the launches traced: 32.6 us -> 31.2 us
  Pallas kernels: 27.8 us -> 26.3 us
    pallas_call x1, Pallas kernels: 15 us -> 13.5 us  [shards(): scoring_call(count, blocks)]
where the time goes in v1:
time: 31.8 us; the launch traced here: 31.2 us
  Pallas kernels  26.3 us (83%)
  local copies, waits for them, and re-layouts  3.23 us (10%)
  other arithmetic  1.56 us (5%)
    pallas_call x1, Pallas kernels, shards(): scoring_call(count, blocks)  13.5 us
    pallas_call x1, Pallas kernels, shards(): pl.pallas_call(body, out_shape=(jax.ShapeDtypeStruct((rows, 2 * FBAND), f...  12.8 us
    dynamic_slice x1, local copies, waits for them, and re-layouts, shards(): lax.dynamic_slice_in_dim(strain, start, piece, 1).reshape(rows, STRIDE)  0.95 us
    dynamic_slice x1, local copies, waits for them, and re-layouts, shards(): lax.dynamic_slice_in_dim(segment_valid, start // SEG, pick * blocks, 1)  0.91 us
    dynamic_slice x1, local copies, waits for them, and re-layouts, shards(): next_valid = lax.dynamic_slice_in_dim(segment_valid, follow // SEG, pick, 1)  0.83 us
    slice x1, other arithmetic, shards(): strain[:, :STRIDE]  0.79 us
    convert_element_type x1, other arithmetic, shards(): bin_edges.astype(jnp.float32)  0.68 us

profile of v1, /device:TPU:0, one launch (start us, length us, event | category | flops | bytes accessed | tf_op | source)
XLA Modules:
  0.0 31.2 jit_solution(3624373107297221574)
XLA Ops:
  0.0 0.0 copy-start.1
  0.0 0.0 copy-start.2
  0.0 0.0 copy-start.3
  0.0 0.0 copy-start
  0.0 0.9 %constant_dynamic-slice_fusion.1 = s32[2,96]{1,0:T(2,128)S(1)} fusion(s32[2,768]{1,0:T(2,128)} %param.10, s32[]{:T(128)S(6)} %select_n.28), kind=kLoop, calls=%fused_computation.3 | loop fusion | bytes 1540 | tf_op jit(solution)/shard_map/dynamic_slice | solution.py:344
  0.9 0.1 pad.8.clone
  1.0 0.7 %convert_element_type.9 = f32[2,15]{1,0:T(2,128)S(1)} convert(s32[2,15]{1,0:T(2,128)} %param.13) | non-fusion elementwise | flops 30 | bytes 240 | tf_op jit(solution)/shard_map/convert_element_type | solution.py:349
  1.7 0.8 %constant_dynamic-slice_fusion = (s32[2,2]{1,0:T(2,128)S(1)}, s32[2,2]{1,0:T(2,128)S(1)}) fusion(s32[2,768]{1,0:T(2,128)} %param.10, s32[]{:T(128)S(6)} %select_n.30), kind=kLoop, calls=%fused_computation.2 | loop fusion | bytes 68 | tf_op jit(solution)/shard_map/dynamic_slice | solution.py:345
  2.5 0.8 %fusion = (f32[2,512]{1,0:T(2,128)S(1)}, f32[2,512]{1,0:T(2,128)S(1)}, f32[2,512]{1,0:T(2,128)S(1)}) fusion(f32[2,196608]{1,0:T(2,128)} %param.9, s32[]{:T(128)S(6)} %select_n.25, f32[2,512]{1,0:T(2,128)} %param.11, s32[2]{0:T(128)} %param.12), kind=kLoop, calls=%fused_computation.6 | loop fusion | flops 2048 | bytes 24588 | tf_op jit(solution)/shard_map/slice | solution.py:343
  3.3 0.1 reshape.11
  3.4 0.1 add_convert_fusion.refs_1_
  3.5 0.9 %constant_dynamic-slice_fusion.3 = f32[2,24576]{1,0:T(2,128)S(1)} fusion(f32[2,196608]{1,0:T(2,128)} %param.9, s32[]{:T(128)S(6)} %select_n.24), kind=kLoop, calls=%fused_computation.5 | loop fusion | bytes 393220 | tf_op jit(solution)/shard_map/dynamic_slice | solution.py:337
  4.5 0.2 reshape.10
  4.7 0.2 concatenate.6.refs_0_
  4.8 0.0 copy-done.1
  4.8 12.8 %shard_map.91 = (f32[96,512]{1,0:T(8,128)S(1)}, f32[16,2,512]{2,1,0:T(2,128)S(1)}, f32[16,2,128]{2,1,0:T(2,128)S(1)}, s32[8,2,128]{2,1,0:T(2,128)S(1)}) custom-call(f32[112,512]{1,0:T(8,128)S(1)} %concatenate.6.refs_0_, f32[112,2]{1,0:T(8,128)S(1)} %add_convert_fusion.refs_1_, f32[2,128]{1,0:T(2,128)S(1)} %pad.4.refs_2_, bf16[2,512,512]{2,1,0:T(8,128)(2,1)S(1)} %copy-done.1), custom_call_target="tpu_custom_call" | custom-call | tf_op jit(solution)/shard_map/pallas_call | solution.py:358
  17.6 0.0 copy-done.2
  17.7 0.0 copy-done.3
  17.7 0.0 copy-done
  17.7 13.5 %shard_map.92 = f32[5,24576]{1,0:T(8,128)} custom-call(s32[16,16]{1,0:T(8,128)S(1)} %bitcast.2, f32[96,512]{1,0:T(8,128)S(1)} %get-tuple-element.10.refs_1_, f32[16,2,512]{2,1,0:T(2,128)S(1)} %get-tuple-element.11.refs_2_, f32[16,2,128]{2,1,0:T(2,128)S(1)} %get-tuple-element.12.refs_3_, bf16[512,1024]{1,0:T(8,128)(2,1)S(1)} %copy-done, ...), custom_call_target="tpu_custom_call" | custom-call | tf_op jit(solution)/shard_map/pallas_call | solution.py:382
  (3 shorter events, 0.0 us)
Async XLA Ops:
  0.0 4.8 %copy-start.1 = (bf16[2,512,512]{2,1,0:T(8,128)(2,1)S(1)}, bf16[2,512,512]{2,1,0:T(8,128)(2,1)}, u32[]{:S(2)}) copy-start(bf16[2,512,512]{2,1,0:T(8,128)(2,1)} %constant.52.clone.refs_3_) | copy-start | bytes 3145732
  0.0 17.6 %copy-start.2 = (bf16[256,512]{1,0:T(8,128)(2,1)S(1)}, bf16[256,512]{1,0:T(8,128)(2,1)}, u32[]{:S(2)}) copy-start(bf16[256,512]{1,0:T(8,128)(2,1)} %constant.55.clone.refs_6_) | copy-start | bytes 786436
  0.0 17.6 %copy-start.3 = (bf16[256,256]{1,0:T(8,128)(2,1)S(1)}, bf16[256,256]{1,0:T(8,128)(2,1)}, u32[]{:S(2)}) copy-start(bf16[256,256]{1,0:T(8,128)(2,1)} %constant.54.clone.refs_5_) | copy-start | bytes 393220
  0.0 17.7 %copy-start = (bf16[512,1024]{1,0:T(8,128)(2,1)S(1)}, bf16[512,1024]{1,0:T(8,128)(2,1)}, u32[]{:S(2)}) copy-start(bf16[512,1024]{1,0:T(8,128)(2,1)} %constant.53.clone.refs_4_) | copy-start | bytes 3145732
